TPU v7x, 32 devices: a whole 2x2x4 slice. The times are simulated.
32 devices in a mesh: row: 4 (over y, x), col: 8 (over z, core).
Axes of the slice: x: 2, y: 2, z: 4, core: 2. Of those that a mesh axis runs over, the one named last changes fastest.
Arguments:
- inputs: bfloat16 [4096, 4096], P('row', 'col'), may hold values from -5 to 5
- norm_gain: float32 [4096], replicated, may hold values from 0.25 to 1.75
- query_train: float32 [4096, 4096], P(('row', 'col')), as said below
- key_train: float32 [4096, 4096], P(('row', 'col')), as said below
- value_train: float32 [4096, 4096], P(('row', 'col')), may hold values from -0.09375 to 0.09375
- out_train: float32 [4096, 2048], P(None, ('row', 'col')), may hold values from -0.09375 to 0.09375
- adapter_down: bfloat16 [4096, 128], replicated, may hold values from -0.09375 to 0.09375
- adapter_up: bfloat16 [128, 3, 32, 128], P(None, None, 'col'), may hold values from -0.5 to 0.5
- lengths: int32 [4, 7], P('row'), may hold values from 1 to 512, 1024 in all within a row
Outputs:
- mixed: bfloat16 [4096, 2048], P(('row', 'col'))
Inputs may be any that keep to these rules, and one draw needn't show every extreme that they name: In each token group the 7 lengths sum to 1024; the longest is 512. `query_train`: entries are of order 1 / sqrt(4096) and at most 32 / sqrt(4096) in magnitude. `key_train`: entries are of order 1 / sqrt(4096) and at most 32 / sqrt(4096) in magnitude.
All inputs are finite; a program needn't handle non-finite values.
Results may differ from a plain program's by a relative error of at most 0.018.
Values may be sent and summed in bfloat16 or wider, within the bound.
A program may use at most 128 MiB of HBM per device.

v0:
```python
import math

import jax
import jax.numpy as jnp
from jax import lax
from jax.sharding import PartitionSpec as P

HEADS = 32
HS = 128
MOST = 512


def segment_of(lengths_row, tok_count):
    position = jnp.arange(tok_count, dtype=jnp.int32)
    order = jnp.arange(lengths_row.shape[0], dtype=jnp.int32)
    prompt_ends = jnp.sum(
        jnp.where(order[:, None] <= order[None, :], lengths_row[:, None], 0), axis=0
    )
    return jnp.sum((position[:, None] >= prompt_ends[None, :]).astype(jnp.int32), axis=1)


def attend(queries, keys_all, values_all, segment, heads):
    tok_count = queries.shape[0]
    block = min(256, tok_count)
    factor = 1.0 / math.sqrt(HS)
    out = []
    for head in range(heads):
        lanes = slice(head * HS, (head + 1) * HS)
        rows = []
        for first in range(0, tok_count, block):
            low = max(0, (first - MOST + 1) // block * block)
            end = first + block
            scores = (
                lax.dot_general(
                    queries[first:end, lanes],
                    keys_all[low:end, lanes],
                    (((1,), (1,)), ((), ())),
                    preferred_element_type=jnp.float32,
                )
                * factor
            )
            query_pos = first + jnp.arange(block, dtype=jnp.int32)
            key_pos = low + jnp.arange(end - low, dtype=jnp.int32)
            allowed = (segment[first:end, None] == segment[None, low:end]) & (
                key_pos[None, :] <= query_pos[:, None]
            )
            scores = jnp.where(allowed, scores, -1e30)
            highest = jnp.max(scores, axis=1, keepdims=True)
            exponent = jnp.exp(scores - highest)
            weights = (exponent / jnp.sum(exponent, axis=1, keepdims=True)).astype(jnp.bfloat16)
            rows.append(
                jnp.dot(
                    weights, values_all[low:end, lanes], preferred_element_type=jnp.float32
                ).astype(jnp.bfloat16)
            )
        out.append(jnp.concatenate(rows, axis=0))
    return jnp.concatenate(out, axis=1)


def on_device(
    inputs,
    norm_gain,
    query_train,
    key_train,
    value_train,
    out_train,
    adapter_down,
    adapter_up,
    lengths,
):
    cols = lax.axis_size("col")
    rows, features = query_train.shape
    heads = HEADS // cols
    width = heads * HS

    def serve(trained):
        half = trained.astype(jnp.bfloat16).reshape(rows, cols, width).transpose(1, 0, 2)
        moved = lax.all_to_all(half, "col", split_axis=0, concat_axis=0)
        return moved.reshape(cols * rows, width)

    parts = []
    for trained in (query_train, key_train, value_train):
        parts.append(lax.all_gather(serve(trained), "row", axis=0, tiled=True))
    whole = lax.all_gather(inputs, "col", axis=1, tiled=True)
    out_half = out_train.astype(jnp.bfloat16).T
    out_half = out_half.reshape(out_half.shape[0], cols, width).transpose(1, 0, 2)
    out_moved = lax.all_to_all(out_half, "col", split_axis=0, concat_axis=0)
    out_t = lax.all_gather(out_moved.reshape(-1, width), "row", axis=0, tiled=True)

    floats = whole.astype(jnp.float32)
    mean_square = jnp.mean(floats * floats, axis=1, keepdims=True)
    normed = (floats * lax.rsqrt(mean_square + 1e-05) * norm_gain).astype(jnp.bfloat16)
    adapted = jnp.dot(normed, adapter_down, preferred_element_type=jnp.float32).astype(jnp.bfloat16)
    projected = []
    for s in range(3):
        up = adapter_up[:, s].reshape(adapter_up.shape[0], width)
        projected.append(
            (
                jnp.dot(normed, parts[s], preferred_element_type=jnp.float32)
                + jnp.dot(adapted, up, preferred_element_type=jnp.float32)
            ).astype(jnp.bfloat16)
        )
    segment = segment_of(lengths[0], normed.shape[0])
    attended = attend(*projected, segment, heads)
    partial_out = lax.dot_general(
        attended, out_t, (((1,), (1,)), ((), ())), preferred_element_type=jnp.float32
    )
    return lax.psum_scatter(
        partial_out.astype(jnp.bfloat16), "col", scatter_dimension=0, tiled=True
    )


def solution(mesh):
    in_specs = (
        P("row", "col"),
        P(),
        P(("row", "col"), None),
        P(("row", "col"), None),
        P(("row", "col"), None),
        P(None, ("row", "col")),
        P(),
        P(None, None, "col", None),
        P("row", None),
    )
    out_specs = P(("row", "col"), None)
    return jax.shard_map(
        on_device, mesh=mesh, in_specs=in_specs, out_specs=out_specs, check_vma=False
    )
```

profile of v0, /device:TPU:8, one launch (start us, length us, event | category | flops | bytes accessed | tf_op | source)
XLA Modules:
  0.0 392.1 jit_solution(3110643182355118537)
XLA Ops:
  6.5 0.7 all-gather.6.cloned.1.call-update
  7.3 1.8 copy.24
  9.2 54.8 %all_to_all.20 = bf16[8,128,512]{1,2,0:T(8,128)(2,1)S(1)} all-to-all(bf16[8,128,512]{1,2,0:T(8,128)(2,1)S(1)} %bitcast.46), channel_id=1, replica_groups=mesh['row'=4,'col'=8] {'col'}, dimensions={0} | all-to-all | bytes 2097152 | tf_op jit(solution)/shard_map/all_to_all | solution.py:78
  63.9 1.3 copy.25
  65.3 1.8 copy.26
  67.2 53.5 %all_to_all.21 = bf16[8,128,512]{1,2,0:T(8,128)(2,1)S(1)} all-to-all(bf16[8,128,512]{1,2,0:T(8,128)(2,1)S(1)} %bitcast.47), channel_id=1, replica_groups=mesh['row'=4,'col'=8] {'col'}, dimensions={0} | all-to-all | bytes 2097152 | tf_op jit(solution)/shard_map/all_to_all | solution.py:78
  120.6 1.3 copy.27
  122.0 1.8 copy.28
  123.9 29.5 %all_to_all.22 = bf16[8,128,512]{1,2,0:T(8,128)(2,1)S(1)} all-to-all(bf16[8,128,512]{1,2,0:T(8,128)(2,1)S(1)} %bitcast.48), channel_id=1, replica_groups=mesh['row'=4,'col'=8] {'col'}, dimensions={0} | all-to-all | bytes 2097152 | tf_op jit(solution)/shard_map/all_to_all | solution.py:78
  153.4 1.3 copy.29
  155.0 0.9 copy.30
  155.9 5.8 %all-to-all-start.3 = ((bf16[8,64,512]{2,1,0:T(8,128)(2,1)}), bf16[8,64,512]{2,1,0:T(8,128)(2,1)S(1)}, u32[]{:S(2)}, u32[]{:S(2)}) async-start(bf16[8,64,512]{2,1,0:T(8,128)(2,1)} %copy.30), calls=%async_computation.3 | async-start | bytes 1048576 | tf_op jit(solution)/shard_map/all_to_all | solution.py:87
  162.2 11.7 %all-to-all-done.3 = bf16[8,64,512]{2,1,0:T(8,128)(2,1)S(1)} async-done(((bf16[8,64,512]{2,1,0:T(8,128)(2,1)}), bf16[8,64,512]{2,1,0:T(8,128)(2,1)S(1)}, u32[]{:S(2)}, u32[]{:S(2)}) %all-to-all-start.3) | async-done | bytes 524320 | tf_op jit(solution)/shard_map/all_to_all | solution.py:87
  173.9 0.8 copy-done.2
  174.8 5.1 %fusion = f32[1024]{0:T(1024)S(1)} fusion(bf16[1024,4096]{1,0:T(8,128)(2,1)} %all-gather.6.cloned.1.call-done), kind=kLoop, calls=%fused_computation.2 | loop fusion | flops 12581888 | bytes 8392704 | tf_op jit(solution)/shard_map/reduce_sum | solution.py:91
  179.9 10.3 %fusion.2 = bf16[1024,4096]{1,0:T(8,128)(2,1)} fusion(bf16[1024,4096]{1,0:T(8,128)(2,1)} %all-gather.6.cloned.1.call-done, f32[4096]{0:T(1024)S(1)} %copy-done.19, f32[1024]{0:T(1024)S(1)} %add_rsqrt_fusion), kind=kLoop, calls=%fused_computation.4 | loop fusion | flops 16777216 | bytes 16797696 | tf_op jit(solution)/shard_map/convert_element_type | solution.py:92
  190.2 5.7 %convolution_convert_fusion.1 = bf16[1024,128]{1,0:T(8,128)(2,1)S(1)} fusion(bf16[1024,4096]{1,0:T(8,128)(2,1)} %fusion.2, bf16[4096,128]{1,0:T(8,128)(2,1)S(1)} %copy-done), kind=kOutput, calls=%fused_computation.33 | convolution fusion | flops 1073872896 | bytes 9699328 | tf_op jit(solution)/shard_map/dot_general | solution.py:93
  196.0 8.6 %fusion.143 = f32[1024,512]{1,0:T(8,128)S(1)} fusion(bf16[1024,4096]{1,0:T(8,128)(2,1)} %fusion.2, bf16[4096,512]{1,0:T(8,128)(2,1)} %all-gather.8.cloned.1.call-done), kind=kOutput, calls=%fused_computation.227 | convolution fusion | flops 4294967296 | bytes 14680064 | tf_op jit(solution)/shard_map/dot_general | solution.py:99
  204.6 0.4 add_convert_fusion.2
  205.0 35.0 %all-gather.10.cloned.1.call-done = bf16[4096,512]{1,0:T(8,128)(2,1)} async-done(((bf16[1024,512]{1,0:T(8,128)(2,1)}), bf16[4096,512]{1,0:T(8,128)(2,1)}) %all-gather.10.cloned.1.call-update) | async-done | bytes 4194320 | tf_op jit(solution)/shard_map/all_gather | solution.py:83
  240.1 8.1 %fusion.144 = f32[1024,512]{1,0:T(8,128)S(1)} fusion(bf16[1024,4096]{1,0:T(8,128)(2,1)} %fusion.2, bf16[4096,512]{1,0:T(8,128)(2,1)} %all-gather.10.cloned.1.call-done), kind=kOutput, calls=%fused_computation.228 | convolution fusion | flops 4294967296 | bytes 14680064 | tf_op jit(solution)/shard_map/dot_general | solution.py:99
  248.2 0.4 add_convert_fusion.1
  248.9 1.5 fusion.138
  250.4 1.7 fusion.141
  252.1 0.9 fusion.137
  252.9 1.9 fusion.140
  254.8 1.0 fusion.136
  255.8 1.8 fusion.139
  257.6 1.6 fusion.135
  259.2 1.4 fusion.134
  260.7 1.6 fusion.133
  262.3 1.8 fusion.132
  264.1 1.7 fusion.131
  265.8 1.4 fusion.130
  267.2 1.6 fusion.129
  268.9 1.2 fusion.128
  270.1 1.2 fusion.127
  271.3 0.6 fusion.65
  271.9 22.6 %all-gather.12.cloned.1.call-done = bf16[4096,512]{1,0:T(8,128)(2,1)} async-done(((bf16[1024,512]{1,0:T(8,128)(2,1)}), bf16[4096,512]{1,0:T(8,128)(2,1)}) %all-gather.12.cloned.1.call-update) | async-done | bytes 4194320 | tf_op jit(solution)/shard_map/all_gather | solution.py:83
  294.5 8.4 %fusion.145 = f32[1024,512]{1,0:T(8,128)S(1)} fusion(bf16[1024,4096]{1,0:T(8,128)(2,1)} %fusion.2, bf16[4096,512]{1,0:T(8,128)(2,1)} %all-gather.12.cloned.1.call-done), kind=kOutput, calls=%fused_computation.229 | convolution fusion | flops 4294967296 | bytes 14680064 | tf_op jit(solution)/shard_map/dot_general | solution.py:99
  302.9 0.4 add_convert_fusion
  303.4 0.5 copy-done.16
  304.5 0.3 copy-done.17
  305.8 0.3 fusion.51
  306.1 0.3 fusion.52
  307.5 0.3 fusion.55
  307.8 0.3 fusion.56
  308.0 0.3 fusion.57
  308.6 0.3 fusion.58
  308.8 0.9 convolution_convert_fusion.13
  309.8 0.9 convolution_convert_fusion.10
  310.7 0.3 convolution_convert_fusion.7
  311.0 0.3 convolution_convert_fusion.4
  311.3 0.4 convolution_convert_fusion.12
  311.7 0.4 convolution_convert_fusion.11
  312.1 0.4 convolution_convert_fusion.9
  312.5 0.4 convolution_convert_fusion.8
  312.9 0.4 convolution_convert_fusion.6
  313.4 0.4 convolution_convert_fusion.5
  313.8 0.4 convolution_convert_fusion.3
  314.2 0.4 convolution_convert_fusion.2
  314.6 16.9 %all-gather.14.cloned.1.call-done = bf16[2048,512]{1,0:T(8,128)(2,1)} async-done(((bf16[512,512]{1,0:T(8,128)(2,1)}), bf16[2048,512]{1,0:T(8,128)(2,1)}) %all-gather.14.cloned.1.call-update) | async-done | bytes 2097168 | tf_op jit(solution)/shard_map/all_gather | solution.py:88
  331.6 7.4 %convolution_convert_fusion = bf16[1024,2048]{1,0:T(8,128)(2,1)} fusion(bf16[2048,512]{1,0:T(8,128)(2,1)} %all-gather.14.cloned.1.call-done, bf16[256,128]{1,0:T(8,128)(2,1)S(1)} %convolution_convert_fusion.2, bf16[256,128]{1,0:T(8,128)(2,1)S(1)} %convolution_convert_fusion.3, bf16[256,128]{1,0:T(8,128)(2,1)S(1)} %convolution_convert_fusion.4, ...), kind=kOutput, calls=%fused_computation.5 | convolution fusion | flops 2166358016 | bytes 7340032 | tf_op jit(solution)/shard_map/dot_general | solution.py:105
  339.0 46.2 %reduce-scatter.2.cloned.1.call-done = bf16[128,2048]{1,0:T(8,128)(2,1)} async-done(((bf16[1024,2048]{1,0:T(8,128)(2,1)}), bf16[128,2048]{1,0:T(8,128)(2,1)}) %reduce-scatter.2.cloned.1.call-update) | async-done | bytes 524304 | tf_op jit(solution)/shard_map/reduce_scatter | solution.py:108
  (143 shorter events, 3.9 us)
Async XLA Ops:
  6.5 183.7 %copy-start = (bf16[4096,128]{1,0:T(8,128)(2,1)S(1)}, bf16[4096,128]{1,0:T(8,128)(2,1)}, u32[]{:S(2)}) copy-start(bf16[4096,128]{1,0:T(8,128)(2,1)} %param.15) | copy-start | bytes 3145732
  6.5 168.2 %all-gather.6.cloned.1.call-start = ((), (), s32[]{:S(2)}) async-start(), calls=%async_computation.5 | async-start | bytes 9437184 | tf_op jit(solution)/shard_map/all_gather | solution.py:84
  7.3 188.7 %all-gather.8.cloned.1.call-start = ((), (), s32[]{:S(2)}) async-start(), calls=%async_computation.6 | async-start | bytes 5242880 | tf_op jit(solution)/shard_map/all_gather | solution.py:83
  65.3 174.8 %all-gather.10.cloned.1.call-start = ((), (), s32[]{:S(2)}) async-start(), calls=%async_computation.7 | async-start | bytes 5242880 | tf_op jit(solution)/shard_map/all_gather | solution.py:83
  122.0 172.5 %all-gather.12.cloned.1.call-start = ((), (), s32[]{:S(2)}) async-start(), calls=%async_computation.8 | async-start | bytes 5242880 | tf_op jit(solution)/shard_map/all_gather | solution.py:83
  153.4 1.3 copy-start.3
  154.7 7.0 %copy-start.44 = (s32[1,7]{1,0:T(1,128)S(1)}, s32[1,7]{1,0:T(1,128)}, u32[]{:S(2)}) copy-start(s32[1,7]{1,0:T(1,128)} %param.17) | copy-start | bytes 88
  154.7 7.3 %copy-start.13 = (bf16[128,3,4,128]{3,2,1,0:T(4,128)(2,1)S(1)}, bf16[128,3,4,128]{3,2,1,0:T(4,128)(2,1)}, u32[]{:S(2)}) copy-start(bf16[128,3,4,128]{3,2,1,0:T(4,128)(2,1)} %param.16) | copy-start | bytes 1179652
  155.9 17.9 %all-to-all-start.3 = ((bf16[8,64,512]{2,1,0:T(8,128)(2,1)}), bf16[8,64,512]{2,1,0:T(8,128)(2,1)S(1)}, u32[]{:S(2)}, u32[]{:S(2)}) async-start(bf16[8,64,512]{2,1,0:T(8,128)(2,1)} %copy.30), calls=%async_computation.3 | async-start | bytes 1048576 | tf_op jit(solution)/shard_map/all_to_all | solution.py:87
  161.7 169.8 %all-gather.14.cloned.1.call-start = ((), (), s32[]{:S(2)}) async-start(), calls=%async_computation.9 | async-start | bytes 2621440 | tf_op jit(solution)/shard_map/all_gather | solution.py:88
  161.7 90.3 %copy-start.49 = (s32[256]{0:T(256)}, s32[256]{0:T(256)S(1)}, u32[]{:S(2)}) copy-start(s32[256]{0:T(256)S(1)} %iota_add_fusion.3) | copy-start | bytes 3076
  161.9 92.9 %copy-start.47 = (s32[256]{0:T(256)}, s32[256]{0:T(256)S(1)}, u32[]{:S(2)}) copy-start(s32[256]{0:T(256)S(1)} %iota_add_fusion.2) | copy-start | bytes 3076
  162.0 93.8 %copy-start.45 = (s32[256]{0:T(256)}, s32[256]{0:T(256)S(1)}, u32[]{:S(2)}) copy-start(s32[256]{0:T(256)S(1)} %iota_add_fusion.1) | copy-start | bytes 3076
  162.0 86.8 %copy-start.42 = (s32[256]{0:T(256)}, s32[256]{0:T(256)S(1)}, u32[]{:S(2)}) copy-start(s32[256]{0:T(256)S(1)} %get-tuple-element.8) | copy-start | bytes 3076
  162.0 90.0 %copy-start.40 = (s32[256]{0:T(256)}, s32[256]{0:T(256)S(1)}, u32[]{:S(2)}) copy-start(s32[256]{0:T(256)S(1)} %get-tuple-element.11) | copy-start | bytes 3076
  162.0 92.8 %copy-start.38 = (s32[256]{0:T(256)}, s32[256]{0:T(256)S(1)}, u32[]{:S(2)}) copy-start(s32[256]{0:T(256)S(1)} %get-tuple-element.10) | copy-start | bytes 3076
  162.0 93.8 %copy-start.36 = (s32[256]{0:T(256)}, s32[256]{0:T(256)S(1)}, u32[]{:S(2)}) copy-start(s32[256]{0:T(256)S(1)} %get-tuple-element.9) | copy-start | bytes 3076
  173.9 0.8 copy-start.2
  174.7 5.2 %copy-start.19 = (f32[4096]{0:T(1024)S(1)}, f32[4096]{0:T(1024)}, u32[]{:S(2)}) copy-start(f32[4096]{0:T(1024)} %param.10) | copy-start | bytes 49156
  174.7 210.6 %reduce-scatter.2.cloned.1.call-start = ((), (), s32[]{:S(2)}) async-start(), calls=%async_computation.10 | async-start | bytes 4718592 | tf_op jit(solution)/shard_map/reduce_scatter | solution.py:108
  248.8 22.5 %copy-start.15 = (f32[256,256]{0,1:T(8,128)}, f32[256,256]{0,1:T(8,128)S(1)}, u32[]{:S(2)}) copy-start(f32[256,256]{0,1:T(8,128)S(1)} %get-tuple-element.45) | copy-start | bytes 786436
  248.9 22.5 %copy-start.31 = (f32[256]{0:T(256)}, f32[256]{0:T(256)S(1)}, u32[]{:S(2)}) copy-start(f32[256]{0:T(256)S(1)} %get-tuple-element.44) | copy-start | bytes 3076
  254.8 4.4 %copy-start.43 = (s32[256]{0:T(256)S(1)}, s32[256]{0:T(256)}, u32[]{:S(2)}) copy-start(s32[256]{0:T(256)} %copy-done.42) | copy-start | bytes 3076
  255.8 4.9 %copy-start.41 = (s32[256]{0:T(256)S(1)}, s32[256]{0:T(256)}, u32[]{:S(2)}) copy-start(s32[256]{0:T(256)} %copy-done.40) | copy-start | bytes 3076
  255.8 4.9 %copy-start.50 = (s32[256]{0:T(256)S(1)}, s32[256]{0:T(256)}, u32[]{:S(2)}) copy-start(s32[256]{0:T(256)} %copy-done.49) | copy-start | bytes 3076
  255.8 6.5 %copy-start.39 = (s32[256]{0:T(256)S(1)}, s32[256]{0:T(256)}, u32[]{:S(2)}) copy-start(s32[256]{0:T(256)} %copy-done.38) | copy-start | bytes 3076
  255.8 6.5 %copy-start.48 = (s32[256]{0:T(256)S(1)}, s32[256]{0:T(256)}, u32[]{:S(2)}) copy-start(s32[256]{0:T(256)} %copy-done.47) | copy-start | bytes 3076
  257.6 6.4 %copy-start.37 = (s32[256]{0:T(256)S(1)}, s32[256]{0:T(256)}, u32[]{:S(2)}) copy-start(s32[256]{0:T(256)} %copy-done.36) | copy-start | bytes 3076
  257.6 6.4 %copy-start.46 = (s32[256]{0:T(256)S(1)}, s32[256]{0:T(256)}, u32[]{:S(2)}) copy-start(s32[256]{0:T(256)} %copy-done.45) | copy-start | bytes 3076
  302.9 1.0 copy-start.16
  302.9 1.0 copy-start.32
  302.9 1.0 copy-start.35
  302.9 1.2 copy-start.14
  302.9 1.2 copy-start.30
  303.9 1.0 copy-start.17
  303.9 1.0 copy-start.33
  303.9 1.3 copy-start.18
  303.9 1.3 copy-start.34
  304.1 1.4 copy-start.10
  304.2 1.4 copy-start.27
  304.2 1.5 copy-start.4
  304.2 1.5 copy-start.22
  304.5 1.6 copy-start.6
  304.5 1.6 copy-start.24
  304.9 1.5 copy-start.26
  305.2 1.5 copy-start.20
  305.3 1.7 copy-start.21
  305.5 1.7 copy-start.11
  305.5 1.7 copy-start.28
  305.8 1.7 copy-start.7
  305.8 1.7 copy-start.25
  306.1 1.6 copy-start.5
  306.1 1.6 copy-start.23
  306.4 1.6 copy-start.8
  306.6 1.7 copy-start.12
  306.7 1.7 copy-start.29
  306.9 1.6 copy-start.9
  314.2 17.4 %copy-start.51 = (bf16[256,128]{1,0:T(8,128)(2,1)S(1)}, bf16[256,128]{1,0:T(8,128)(2,1)}, u32[]{:S(2)}) copy-start(bf16[256,128]{1,0:T(8,128)(2,1)} %convolution_convert_fusion.13) | copy-start | bytes 196612
  314.2 17.3 %copy-start.52 = (bf16[256,128]{1,0:T(8,128)(2,1)S(1)}, bf16[256,128]{1,0:T(8,128)(2,1)}, u32[]{:S(2)}) copy-start(bf16[256,128]{1,0:T(8,128)(2,1)} %convolution_convert_fusion.10) | copy-start | bytes 196612
  339.0 46.3 %copy-start.1 = (bf16[4096,128]{1,0:T(8,128)(2,1)S(1)}, bf16[4096,128]{1,0:T(8,128)(2,1)}, u32[]{:S(2)}) copy-start(bf16[4096,128]{1,0:T(8,128)(2,1)} %param.15) | copy-start | bytes 3145732
Sparse Core Ops, SparseCore 0:
  9.0 118.4 all-gather.5
  129.3 56.1 all-gather.7
  187.3 52.6 all-gather.9
  241.8 52.7 all-gather.11
  296.2 35.3 all-gather.13
  339.2 46.0 reduce-scatter.1
where the time goes:
time: 398 us; the launch traced here: 392 us
  blocking collectives  138 us (35%)
  waiting for transfers between devices  133 us (33%)
  matrix products  68.8 us (17%)
  other arithmetic  19.5 us (5%)
  between operations  14.3 us (4%)
  local copies, waits for them, and re-layouts  12.5 us (3%)
  starting transfers between devices  5.97 us (2%)
    all_to_all x3, blocking collectives, serve(): moved = lax.all_to_all(half, 'col', split_axis=0, concat_axis=0)  138 us
    all_gather x3, waiting for transfers between devices, on_device(): parts.append(lax.all_gather(serve(trained), 'row', axis=0, tiled=True))  57.7 us
    reduce_scatter x1, waiting for transfers between devices, on_device(): lax.psum_scatter(partial_out.astype(jnp.bfloat16), 'col', scatter_dimensi...  46.2 us
    dot_general x3, matrix products, on_device(): jnp.dot(normed, parts[s], preferred_element_type=jnp.float32)  25.1 us
    dot_general x16, matrix products, attend(): lax.dot_general(queries[first:end, lanes], keys_all[low:end, lanes], (((1...  22.6 us
    all_gather x1, waiting for transfers between devices, on_device(): lax.all_gather(out_moved.reshape(-1, width), 'row', axis=0, tiled=True)  16.9 us
    all_to_all x1, waiting for transfers between devices, on_device(): out_moved = lax.all_to_all(out_half, 'col', split_axis=0, concat_axis=0)  11.7 us
    convert_element_type x1, other arithmetic, on_device(): (floats * lax.rsqrt(mean_square + 1e-05) * norm_gain).astype(jnp.bfloat16)  10.3 us
  transfers between devices with their start and end apart: 7, of which 5 were waited for; matrix products, arithmetic and copies ran while one was open for 23% of the time, Pallas kernels for 0%

commit v1 on v0

--- a/solution.py
+++ b/solution.py
@@ -1,8 +1,11 @@
+import functools
 import math
 
 import jax
 import jax.numpy as jnp
 from jax import lax
+from jax.experimental import pallas as pl
+from jax.experimental.pallas import tpu as pltpu
 from jax.sharding import PartitionSpec as P
 
 HEADS = 32
@@ -57,6 +60,262 @@
     return jnp.concatenate(out, axis=1)
 
 
+def move_kernel(
+    row_n,
+    col_n,
+    x,
+    w0,
+    w1,
+    w2,
+    w3,
+    whole,
+    d0,
+    d1,
+    d2,
+    d3,
+    local_sem,
+    a_send,
+    a_recv,
+    r_send,
+    r_recv,
+    g_send,
+    g_recv,
+    c_send,
+    c_recv,
+    s_send,
+    s_recv,
+):
+    src, dst = (w0, w1, w2, w3), (d0, d1, d2, d3)
+    r, c = lax.axis_index("row"), lax.axis_index("col")
+    chain = col_n // 2
+    place, core = c // 2, c % 2
+    sibling = c + 1 - 2 * core
+    square = row_n == 4
+    feats = x.shape[1]
+
+    barrier = pltpu.get_barrier_semaphore()
+
+    def greet_col(off, carry):
+        pl.semaphore_signal(barrier, inc=1, device_id={"col": (c + off) % col_n})
+        return carry
+
+    def greet_row(off, carry):
+        pl.semaphore_signal(barrier, inc=1, device_id={"row": (r + off) % row_n})
+        return carry
+
+    lax.fori_loop(1, col_n, greet_col, 0)
+    lax.fori_loop(1, row_n, greet_row, 0)
+    pl.semaphore_wait(barrier, col_n - 1 + row_n - 1)
+
+    def a_copy(i, off):
+        return pltpu.make_async_remote_copy(
+            src_ref=src[i].at[(c + off) % col_n],
+            dst_ref=dst[i].at[r * col_n + c],
+            send_sem=a_send.at[i, off],
+            recv_sem=a_recv.at[i, off],
+            device_id={"col": (c + off) % col_n},
+        )
+
+    def a_start(i):
+        def one(off, carry):
+            a_copy(i, off).start()
+            return carry
+
+        lax.fori_loop(1, col_n, one, 0)
+
+    def peer_of(way):
+        if square:
+            return (r + 1 - 2 * (r % 2)) if way == 0 else (r + 2) % 4
+        return (r + 1 + way) % row_n
+
+    ways = 2 if square else row_n - 1
+
+    def r_copy(i, way, off, own):
+        origin = (c - off + col_n) % col_n
+        slot = r * col_n + origin
+        return pltpu.make_async_remote_copy(
+            src_ref=src[i].at[c] if own else dst[i].at[slot],
+            dst_ref=dst[i].at[slot],
+            send_sem=r_send.at[i, way, off],
+            recv_sem=r_recv.at[i, way, off],
+            device_id={"row": peer_of(way)},
+        )
+
+    def rows(i):
+        for way in range(ways):
+            r_copy(i, way, 0, True).start()
+
+        def one(off, carry):
+            a_copy(i, off).wait_recv()
+            for way in range(ways):
+                r_copy(i, way, off, False).start()
+            return carry
+
+        lax.fori_loop(1, col_n, one, 0)
+
+    def g_copy(i, way, off):
+        origin = (c - off + col_n) % col_n
+        slot = peer_of(way) * col_n + origin
+        half = src[i].shape[1] // 2
+        part = pl.ds(way * half, half)
+        return pltpu.make_async_remote_copy(
+            src_ref=dst[i].at[slot, part],
+            dst_ref=dst[i].at[slot, part],
+            send_sem=g_send.at[i, way, off],
+            recv_sem=g_recv.at[i, way, off],
+            device_id={"row": peer_of(1 - way)},
+        )
+
+    def diag(i):
+        def one(off, carry):
+            for way in range(ways):
+                r_copy(i, way, off, False).wait_recv()
+                if square:
+                    g_copy(i, way, off).start()
+            return carry
+
+        lax.fori_loop(0, col_n, one, 0)
+
+    def feats_of(block, which):
+        return pl.ds(pl.multiple_of((2 * block + which) * feats, feats), feats)
+
+    def c_copy(way, t):
+        block = place - t if way == 0 else place + t
+        return pltpu.make_async_remote_copy(
+            src_ref=x if t == 0 else whole.at[:, feats_of(block, core)],
+            dst_ref=whole.at[:, feats_of(block, core)],
+            send_sem=c_send.at[way, t],
+            recv_sem=c_recv.at[way, t],
+            device_id={"col": c + 2 if way == 0 else c - 2},
+        )
+
+    def s_copy(way, t):
+        block = place - t if way == 0 else place + t
+        return pltpu.make_async_remote_copy(
+            src_ref=x if t == 0 else whole.at[:, feats_of(block, core)],
+            dst_ref=whole.at[:, feats_of(block, core)],
+            send_sem=s_send.at[way, t],
+            recv_sem=s_recv.at[way, t],
+            device_id={"col": sibling},
+        )
+
+    def held(way, t):
+        return place >= t if way == 0 else place + t < chain
+
+    def onward(way, t):
+        return held(way, t) & ((place + 1 < chain) if way == 0 else (place >= 1))
+
+    def step(t):
+        for way in range(2):
+            if t >= 1:
+
+                @pl.when(held(way, t))
+                def _(way=way):
+                    c_copy(way, t - 1).wait_recv()
+
+            if t + 1 < chain:
+
+                @pl.when(onward(way, t))
+                def _(way=way):
+                    c_copy(way, t).start()
+
+            if t >= 1 or way == 0:
+
+                @pl.when(held(way, t))
+                def _(way=way):
+                    s_copy(way, t).start()
+
+    own = [
+        pltpu.make_async_copy(src[i].at[c], dst[i].at[r * col_n + c], local_sem.at[i])
+        for i in range(4)
+    ]
+    own.append(pltpu.make_async_copy(x, whole.at[:, feats_of(place, core)], local_sem.at[4]))
+    a_start(0)
+    a_start(1)
+    for copy in own:
+        copy.start()
+    rows(0)
+    a_start(2)
+    step(0)
+    rows(1)
+    diag(0)
+    a_start(3)
+    step(1)
+    rows(2)
+    diag(1)
+    if chain > 2:
+        step(2)
+    rows(3)
+    diag(2)
+    for t in range(3, chain):
+        step(t)
+    diag(3)
+
+    for copy in own:
+        copy.wait()
+
+    def finish(i):
+        def one(off, carry):
+            for way in range(ways):
+                r_copy(i, way, off, False).wait_send()
+                if square:
+                    g_copy(i, way, off).wait()
+            return carry
+
+        def two(off, carry):
+            a_copy(i, off).wait_send()
+            return carry
+
+        lax.fori_loop(0, col_n, one, 0)
+        lax.fori_loop(1, col_n, two, 0)
+
+    for i in range(4):
+        finish(i)
+    for t in range(chain):
+        for way in range(2):
+            if t + 1 < chain:
+
+                @pl.when(onward(way, t))
+                def _(way=way, t=t):
+                    c_copy(way, t).wait_send()
+
+            if t >= 1 or way == 0:
+
+                @pl.when(held(way, t))
+                def _(way=way, t=t):
+                    s_copy(way, t).wait()
+
+
+def move(row_n, col_n, x, *blocks):
+    tok_count, feats = x.shape
+    chain = col_n // 2
+    ways = 2 if row_n == 4 else row_n - 1
+    shapes = [jax.ShapeDtypeStruct((tok_count, col_n * feats), x.dtype)] + [
+        jax.ShapeDtypeStruct((row_n * col_n,) + b.shape[1:], b.dtype) for b in blocks
+    ]
+    dma = pltpu.SemaphoreType.DMA
+    return pl.pallas_call(
+        functools.partial(move_kernel, row_n, col_n),
+        out_shape=shapes,
+        in_specs=[pl.BlockSpec(memory_space=pl.ANY)] * 5,
+        out_specs=[pl.BlockSpec(memory_space=pl.ANY)] * 5,
+        scratch_shapes=[
+            dma((5,)),
+            dma((4, col_n)),
+            dma((4, col_n)),
+            dma((4, ways, col_n)),
+            dma((4, ways, col_n)),
+            dma((4, 2, col_n)),
+            dma((4, 2, col_n)),
+            dma((2, chain)),
+            dma((2, chain)),
+            dma((2, chain)),
+            dma((2, chain)),
+        ],
+        compiler_params=pltpu.CompilerParams(collective_id=0, has_side_effects=True),
+    )(x, *blocks)
+
+
 def on_device(
     inputs,
     norm_gain,
@@ -74,18 +333,21 @@
     width = heads * HS
 
     def serve(trained):
-        half = trained.astype(jnp.bfloat16).reshape(rows, cols, width).transpose(1, 0, 2)
-        moved = lax.all_to_all(half, "col", split_axis=0, concat_axis=0)
-        return moved.reshape(cols * rows, width)
-
-    parts = []
-    for trained in (query_train, key_train, value_train):
-        parts.append(lax.all_gather(serve(trained), "row", axis=0, tiled=True))
-    whole = lax.all_gather(inputs, "col", axis=1, tiled=True)
+        return trained.astype(jnp.bfloat16).reshape(rows, cols, width).transpose(1, 0, 2)
+
     out_half = out_train.astype(jnp.bfloat16).T
     out_half = out_half.reshape(out_half.shape[0], cols, width).transpose(1, 0, 2)
-    out_moved = lax.all_to_all(out_half, "col", split_axis=0, concat_axis=0)
-    out_t = lax.all_gather(out_moved.reshape(-1, width), "row", axis=0, tiled=True)
+    whole, *parts = move(
+        lax.axis_size("row"),
+        cols,
+        inputs,
+        serve(query_train),
+        serve(key_train),
+        serve(value_train),
+        out_half,
+    )
+    parts = [part.reshape(-1, width) for part in parts]
+    out_t = parts[3]
 
     floats = whole.astype(jnp.float32)
     mean_square = jnp.mean(floats * floats, axis=1, keepdims=True)

time: 398 us -> 303 us (0.76)
  Pallas kernels: 0 us -> 168 us
  blocking collectives: 138 us -> 0 us
  waiting for transfers between devices: 133 us -> 45.2 us
  matrix products: 68.8 us -> 37.8 us
  starting transfers between devices: 5.97 us -> 0.01 us
    pallas_call x0 -> x1, Pallas kernels: none -> 168 us  [move(): pl.pallas_call(functools.partial(move_kernel, row_n, col_n), out_shape=sh...]
    all_to_all x3 -> x0, blocking collectives: 138 us -> none  [serve(): moved = lax.all_to_all(half, 'col', split_axis=0, concat_axis=0)]
    all_gather x5 -> x0, waiting for transfers between devices: 74.6 us -> none  [the longest x3 57.7 us: on_device(): parts.append(lax.all_gather(serve(trained), 'row', axis=0, tiled=True))]
    dot_general x16, matrix products: 22.6 us -> 5.51 us  [attend(): lax.dot_general(queries[first:end, lanes], keys_all[low:end, lanes], (((1...]
    all_to_all x1 -> x0, waiting for transfers between devices: 11.7 us -> none  [on_device(): out_moved = lax.all_to_all(out_half, 'col', split_axis=0, concat_axis=0)]
    dot_general x3, matrix products: 25.1 us -> 17.4 us  [on_device(): jnp.dot(normed, parts[s], preferred_element_type=jnp.float32)]
    all_to_all x1 -> x0, starting transfers between devices: 5.8 us -> none  [on_device(): out_moved = lax.all_to_all(out_half, 'col', split_axis=0, concat_axis=0)]
    reshape x0 -> x4, local copies, waits for them, and re-layouts: none -> 4.87 us  [the longest x3 4.03 us: serve(): trained.astype(jnp.bfloat16).reshape(rows, cols, width).transpose(1, 0, 2)]
  transfers between devices with their start and end apart: 7 -> 1, of which waited for: 5 -> 1; matrix products, arithmetic and copies ran while one was open for 23% -> 0% of each run, Pallas kernels for 0% -> 0%
where the time goes in v1:
time: 303 us; the launch traced here: 297 us
  Pallas kernels  168 us (55%)
  waiting for transfers between devices  45.2 us (15%)
  matrix products  37.8 us (12%)
  other arithmetic  19.9 us (7%)
  between operations  13.7 us (5%)
  local copies, waits for them, and re-layouts  12.6 us (4%)
    pallas_call x1, Pallas kernels, move(): pl.pallas_call(functools.partial(move_kernel, row_n, col_n), out_shape=sh...  168 us
    reduce_scatter x1, waiting for transfers between devices, on_device(): lax.psum_scatter(partial_out.astype(jnp.bfloat16), 'col', scatter_dimensi...  45.2 us
    dot_general x3, matrix products, on_device(): jnp.dot(normed, parts[s], preferred_element_type=jnp.float32)  17.4 us
    convert_element_type x1, other arithmetic, on_device(): (floats * lax.rsqrt(mean_square + 1e-05) * norm_gain).astype(jnp.bfloat16)  10.3 us
    unnamed x21, local copies, waits for them, and re-layouts  7.56 us
  transfers between devices with their start and end apart: 1, of which 1 were waited for; matrix products, arithmetic and copies ran while one was open for 0% of the time, Pallas kernels for 0%

profile of v1, /device:TPU:8, one launch (start us, length us, event | category | flops | bytes accessed | tf_op | source)
XLA Modules:
  0.0 296.8 jit_solution(866434162319416558)
XLA Ops:
  6.5 0.8 select_reduce_fusion
  7.5 1.8 copy.17
  9.4 1.4 copy.18
  10.8 1.8 copy.19
  12.6 1.3 copy.20
  13.9 1.9 copy.21
  15.8 1.3 copy.22
  17.2 0.8 copy.41
  18.1 167.6 %shard_map.91 = (bf16[1024,4096]{1,0:T(8,128)(2,1)}, bf16[32,128,512]{2,1,0:T(8,128)(2,1)}, bf16[32,128,512]{2,1,0:T(8,128)(2,1)}, bf16[32,128,512]{2,1,0:T(8,128)(2,1)}, bf16[32,64,512]{2,1,0:T(8,128)(2,1)}) custom-call(bf16[1024,512]{1,0:T(8,128)(2,1)} %x.1, bf16[8,128,512]{2,1,0:T(8,128)(2,1)} %bitcast.49, bf16[8,128,512]{2,1,0:T(8,128)(2,1)} %bitcast.50, ...), custom_call_target="tpu_custom_call" | custom-call | tf_op jit(solution)/shard_map/pallas_call | solution.py:297
  185.7 5.1 %fusion = f32[1024]{0:T(1024)S(1)} fusion(bf16[1024,4096]{1,0:T(8,128)(2,1)} %get-tuple-element.10), kind=kLoop, calls=%fused_computation.2 | loop fusion | flops 12581888 | bytes 8392704 | tf_op jit(solution)/shard_map/reduce_sum | solution.py:353
  190.8 10.3 %fusion.2 = bf16[1024,4096]{1,0:T(8,128)(2,1)} fusion(bf16[1024,4096]{1,0:T(8,128)(2,1)} %get-tuple-element.10, f32[4096]{0:T(1024)S(1)} %copy-done.5, f32[1024]{0:T(1024)S(1)} %add_rsqrt_fusion), kind=kLoop, calls=%fused_computation.4 | loop fusion | flops 16777216 | bytes 16797696 | tf_op jit(solution)/shard_map/convert_element_type | solution.py:354
  201.1 8.4 %fusion.143 = f32[1024,512]{1,0:T(8,128)S(1)} fusion(bf16[1024,4096]{1,0:T(8,128)(2,1)} %fusion.2, bf16[4096,512]{1,0:T(8,128)(2,1)} %bitcast.59), kind=kOutput, calls=%fused_computation.228 | convolution fusion | flops 4294967296 | bytes 14680064 | tf_op jit(solution)/shard_map/dot_general | solution.py:361
  209.6 2.3 convolution_convert_fusion.1
  212.1 4.5 %fusion.144 = f32[1024,512]{1,0:T(8,128)S(1)} fusion(bf16[1024,4096]{1,0:T(8,128)(2,1)S(1)} %copy-done.2, bf16[4096,512]{1,0:T(8,128)(2,1)S(1)} %bitcast.58), kind=kOutput, calls=%fused_computation.229 | convolution fusion | flops 4294967296 | bytes 14680064 | tf_op jit(solution)/shard_map/dot_general | solution.py:361
  216.6 0.4 add_convert_fusion.2
  217.0 0.4 add_convert_fusion.1
  217.5 0.2 fusion.142
  217.9 0.3 fusion.141
  218.2 0.3 fusion.137
  218.6 0.4 fusion.140
  219.0 0.4 fusion.136
  219.4 0.4 fusion.139
  219.8 0.4 fusion.135
  220.2 0.2 fusion.134
  220.4 0.3 fusion.133
  220.8 0.4 fusion.132
  221.2 0.4 fusion.131
  221.6 0.2 fusion.130
  221.8 0.3 fusion.129
  222.2 0.4 fusion.128
  222.6 0.4 fusion.127
  223.0 1.0 copy-done.6
  224.0 4.5 %fusion.145 = f32[1024,512]{1,0:T(8,128)S(1)} fusion(bf16[1024,4096]{1,0:T(8,128)(2,1)S(1)} %copy-done.2, bf16[4096,512]{1,0:T(8,128)(2,1)S(1)} %bitcast.57), kind=kOutput, calls=%fused_computation.230 | convolution fusion | flops 4294967296 | bytes 14680064 | tf_op jit(solution)/shard_map/dot_general | solution.py:361
  228.5 0.3 fusion.65
  228.8 0.4 add_convert_fusion
  229.2 0.2 convolution_convert_fusion.17
  229.5 0.2 fusion.60
  229.7 0.3 convolution_convert_fusion.13
  230.0 0.3 fusion.51
  230.3 0.4 convolution_convert_fusion.12
  230.7 0.3 fusion.52
  230.9 0.4 convolution_convert_fusion.11
  231.4 0.2 convolution_convert_fusion.16
  231.7 0.2 fusion.61
  231.9 0.3 convolution_convert_fusion.10
  232.2 0.3 fusion.53
  232.5 0.4 convolution_convert_fusion.9
  232.9 0.3 fusion.54
  233.1 0.4 convolution_convert_fusion.8
  233.6 0.2 convolution_convert_fusion.15
  234.1 0.3 convolution_convert_fusion.7
  234.4 0.3 fusion.55
  234.7 0.4 convolution_convert_fusion.6
  235.1 0.3 fusion.56
  235.3 0.4 convolution_convert_fusion.5
  235.8 0.2 convolution_convert_fusion.14
  236.3 0.3 convolution_convert_fusion.4
  236.6 0.3 fusion.57
  236.9 0.4 convolution_convert_fusion.3
  237.3 0.3 fusion.58
  237.5 0.4 convolution_convert_fusion.2
  237.9 0.9 copy-done.8
  238.9 5.9 %convolution_convert_fusion = bf16[1024,2048]{1,0:T(8,128)(2,1)} fusion(bf16[2048,512]{1,0:T(8,128)(2,1)S(1)} %bitcast.60, bf16[256,128]{1,0:T(8,128)(2,1)S(1)} %convolution_convert_fusion.2, bf16[256,128]{1,0:T(8,128)(2,1)S(1)} %convolution_convert_fusion.3, bf16[256,128]{1,0:T(8,128)(2,1)S(1)} %convolution_convert_fusion.4, ...), kind=kOutput, calls=%fused_computation.5 | convolution fusion | flops 2166358016 | bytes 7340032 | tf_op jit(solution)/shard_map/dot_general | solution.py:367
  244.8 45.2 %reduce-scatter.2.cloned.1.call-done = bf16[128,2048]{1,0:T(8,128)(2,1)} async-done(((bf16[1024,2048]{1,0:T(8,128)(2,1)}), bf16[128,2048]{1,0:T(8,128)(2,1)}) %reduce-scatter.2.cloned.1.call-update) | async-done | bytes 524304 | tf_op jit(solution)/shard_map/reduce_scatter | solution.py:370
  (33 shorter events, 1.2 us)
Async XLA Ops:
  6.5 203.1 %copy-start = (bf16[4096,128]{1,0:T(8,128)(2,1)S(1)}, bf16[4096,128]{1,0:T(8,128)(2,1)}, u32[]{:S(2)}) copy-start(bf16[4096,128]{1,0:T(8,128)(2,1)} %param.15) | copy-start | bytes 3145732
  6.5 283.4 %reduce-scatter.2.cloned.1.call-start = ((), (), s32[]{:S(2)}) async-start(), calls=%async_computation.1 | async-start | bytes 4718592 | tf_op jit(solution)/shard_map/reduce_scatter | solution.py:370
  13.9 3.3 %copy-start.3 = (f32[4096,64]{0,1:T(8,128)S(1)}, f32[4096,64]{0,1:T(8,128)}, u32[]{:S(2)}) copy-start(f32[4096,64]{0,1:T(8,128)} %param.14) | copy-start | bytes 3145732
  185.7 5.1 %copy-start.5 = (f32[4096]{0:T(1024)S(1)}, f32[4096]{0:T(1024)}, u32[]{:S(2)}) copy-start(f32[4096]{0:T(1024)} %param.10) | copy-start | bytes 49156
  201.1 8.5 %copy-start.2 = (bf16[1024,4096]{1,0:T(8,128)(2,1)S(1)}, bf16[1024,4096]{1,0:T(8,128)(2,1)}, u32[]{:S(2)}) copy-start(bf16[1024,4096]{1,0:T(8,128)(2,1)} %fusion.2) | copy-start | bytes 25165828
  209.6 2.4 copy-start.4
  209.6 2.5 copy-start.7
  221.8 2.2 copy-start.6
  237.3 1.6 copy-start.8
  244.7 45.2 %copy-start.1 = (bf16[4096,128]{1,0:T(8,128)(2,1)S(1)}, bf16[4096,128]{1,0:T(8,128)(2,1)}, u32[]{:S(2)}) copy-start(bf16[4096,128]{1,0:T(8,128)(2,1)} %param.15) | copy-start | bytes 3145732
Sparse Core Ops, SparseCore 0:
  244.9 45.0 reduce-scatter.1

commit v2 on v1

--- a/solution.py
+++ b/solution.py
@@ -22,42 +22,222 @@
     return jnp.sum((position[:, None] >= prompt_ends[None, :]).astype(jnp.int32), axis=1)
 
 
-def attend(queries, keys_all, values_all, segment, heads):
-    tok_count = queries.shape[0]
-    block = min(256, tok_count)
+def tail_kernel(
+    order,
+    queries,
+    keys,
+    values,
+    out_t,
+    seg_col,
+    seg_row,
+    mixed,
+    attended,
+    partial,
+    sib_in,
+    from_low,
+    from_high,
+    sib_send,
+    sib_recv,
+    chain_send,
+    low_recv,
+    high_recv,
+):
+    c = lax.axis_index("col")
+    chain = len(order)
+    place, core = c // 2, c % 2
+    sibling = c + 1 - 2 * core
+    tok_count, width = queries.shape
+    pair = tok_count // chain
+    rows = pair // 2
+    model = out_t.shape[0]
+    step = min(512, model)
     factor = 1.0 / math.sqrt(HS)
-    out = []
-    for head in range(heads):
-        lanes = slice(head * HS, (head + 1) * HS)
-        rows = []
-        for first in range(0, tok_count, block):
-            low = max(0, (first - MOST + 1) // block * block)
-            end = first + block
+
+    barrier = pltpu.get_barrier_semaphore()
+    pl.semaphore_signal(barrier, inc=1, device_id={"col": sibling})
+
+    @pl.when(place >= 1)
+    def _():
+        pl.semaphore_signal(barrier, inc=1, device_id={"col": c - 2})
+
+    @pl.when(place + 1 < chain)
+    def _():
+        pl.semaphore_signal(barrier, inc=1, device_id={"col": c + 2})
+
+    ends = (place == 0) | (place == chain - 1)
+
+    @pl.when(ends)
+    def _():
+        pl.semaphore_wait(barrier, 2)
+
+    @pl.when(jnp.logical_not(ends))
+    def _():
+        pl.semaphore_wait(barrier, 3)
+
+    def swap(j):
+        return pltpu.make_async_remote_copy(
+            src_ref=partial.at[j, 1 - core],
+            dst_ref=sib_in.at[j],
+            send_sem=sib_send.at[j],
+            recv_sem=sib_recv.at[j],
+            device_id={"col": sibling},
+        )
+
+    def up(j):
+        return pltpu.make_async_remote_copy(
+            src_ref=partial.at[j, core],
+            dst_ref=from_low.at[j],
+            send_sem=chain_send.at[j],
+            recv_sem=low_recv.at[j],
+            device_id={"col": c + 2},
+        )
+
+    def down(j):
+        return pltpu.make_async_remote_copy(
+            src_ref=partial.at[j, core],
+            dst_ref=from_high.at[j],
+            send_sem=chain_send.at[j],
+            recv_sem=high_recv.at[j],
+            device_id={"col": c - 2},
+        )
+
+    def compute(j):
+        first = j * pair
+        end = first + pair
+        low = max(0, (first - MOST + 1) // pair * pair)
+        shape = (pair, end - low)
+        query_pos = first + lax.broadcasted_iota(jnp.int32, shape, 0)
+        key_pos = low + lax.broadcasted_iota(jnp.int32, shape, 1)
+        allowed = (seg_col[first:end, :] == seg_row[:, low:end]) & (key_pos <= query_pos)
+
+        def head(h, carry):
+            lanes = pl.ds(pl.multiple_of(h * HS, HS), HS)
             scores = (
                 lax.dot_general(
                     queries[first:end, lanes],
-                    keys_all[low:end, lanes],
+                    keys[low:end, lanes],
                     (((1,), (1,)), ((), ())),
                     preferred_element_type=jnp.float32,
                 )
                 * factor
             )
-            query_pos = first + jnp.arange(block, dtype=jnp.int32)
-            key_pos = low + jnp.arange(end - low, dtype=jnp.int32)
-            allowed = (segment[first:end, None] == segment[None, low:end]) & (
-                key_pos[None, :] <= query_pos[:, None]
-            )
             scores = jnp.where(allowed, scores, -1e30)
-            highest = jnp.max(scores, axis=1, keepdims=True)
-            exponent = jnp.exp(scores - highest)
-            weights = (exponent / jnp.sum(exponent, axis=1, keepdims=True)).astype(jnp.bfloat16)
-            rows.append(
-                jnp.dot(
-                    weights, values_all[low:end, lanes], preferred_element_type=jnp.float32
-                ).astype(jnp.bfloat16)
-            )
-        out.append(jnp.concatenate(rows, axis=0))
-    return jnp.concatenate(out, axis=1)
+            exponent = jnp.exp(scores - jnp.max(scores, axis=1, keepdims=True))
+            inverse = 1.0 / jnp.sum(exponent, axis=1, keepdims=True)
+            weights = (exponent * inverse).astype(jnp.bfloat16)
+            attended[:, lanes] = jnp.dot(
+                weights, values[low:end, lanes], preferred_element_type=jnp.float32
+            ).astype(jnp.bfloat16)
+            return carry
+
+        lax.fori_loop(0, width // HS, head, 0)
+
+        def piece(n, carry):
+            cut = pl.ds(pl.multiple_of(n * step, step), step)
+            product = lax.dot_general(
+                attended[...],
+                out_t[cut, :],
+                (((1,), (1,)), ((), ())),
+                preferred_element_type=jnp.float32,
+            ).astype(jnp.bfloat16)
+            partial[j, 0, :, cut] = product[:rows]
+            partial[j, 1, :, cut] = product[rows:]
+            return carry
+
+        lax.fori_loop(0, model // step, piece, 0)
+        swap(j).start()
+
+    def add(j, other):
+        mine = partial[j, core].astype(jnp.float32)
+        partial[j, core] = (mine + other[j].astype(jnp.float32)).astype(jnp.bfloat16)
+
+    def on_chip(j):
+        swap(j).wait()
+        add(j, sib_in)
+        if j > 0:
+
+            @pl.when(place == 0)
+            def _():
+                up(j).start()
+
+        if j < chain - 1:
+
+            @pl.when(place == chain - 1)
+            def _():
+                down(j).start()
+
+    for index, j in enumerate(order):
+        compute(j)
+        if index > 0:
+            on_chip(order[index - 1])
+    on_chip(order[-1])
+
+    for hop in range(1, chain - 1):
+        for j in order:
+            if hop < j:
+
+                @pl.when(place == hop)
+                def _(j=j):
+                    up(j).wait_recv()
+                    add(j, from_low)
+                    up(j).start()
+
+            if chain - 1 - hop > j:
+
+                @pl.when(place == chain - 1 - hop)
+                def _(j=j):
+                    down(j).wait_recv()
+                    add(j, from_high)
+                    down(j).start()
+
+    for j in range(chain):
+
+        @pl.when(place == j)
+        def _(j=j):
+            total = partial[j, core].astype(jnp.float32)
+            if j > 0:
+                up(j).wait_recv()
+                total = total + from_low[j].astype(jnp.float32)
+            if j < chain - 1:
+                down(j).wait_recv()
+                total = total + from_high[j].astype(jnp.float32)
+            mixed[...] = total.astype(jnp.bfloat16)
+
+        @pl.when(place != j)
+        def _(j=j):
+            up(j).wait_send()
+
+
+def tail(col_n, queries, keys, values, out_t, segment):
+    tok_count = queries.shape[0]
+    model, width = out_t.shape
+    chain = col_n // 2
+    rows = tok_count // col_n
+    order = []
+    for near in range((chain + 1) // 2):
+        order += [chain - 1 - near] + ([near] if near != chain - 1 - near else [])
+    dma = pltpu.SemaphoreType.DMA
+    return pl.pallas_call(
+        functools.partial(tail_kernel, tuple(order)),
+        out_shape=jax.ShapeDtypeStruct((rows, model), jnp.bfloat16),
+        in_specs=[pl.BlockSpec(memory_space=pltpu.VMEM)] * 6,
+        out_specs=pl.BlockSpec(memory_space=pltpu.VMEM),
+        scratch_shapes=[
+            pltpu.VMEM((2 * rows, width), jnp.bfloat16),
+            pltpu.VMEM((chain, 2, rows, model), jnp.bfloat16),
+            pltpu.VMEM((chain, rows, model), jnp.bfloat16),
+            pltpu.VMEM((chain, rows, model), jnp.bfloat16),
+            pltpu.VMEM((chain, rows, model), jnp.bfloat16),
+            dma((chain,)),
+            dma((chain,)),
+            dma((chain,)),
+            dma((chain,)),
+            dma((chain,)),
+        ],
+        compiler_params=pltpu.CompilerParams(
+            collective_id=1, has_side_effects=True, vmem_limit_bytes=44 * 2**20
+        ),
+    )(queries, keys, values, out_t, segment[:, None], segment[None, :])
 
 
 def move_kernel(
@@ -363,13 +543,7 @@
             ).astype(jnp.bfloat16)
         )
     segment = segment_of(lengths[0], normed.shape[0])
-    attended = attend(*projected, segment, heads)
-    partial_out = lax.dot_general(
-        attended, out_t, (((1,), (1,)), ((), ())), preferred_element_type=jnp.float32
-    )
-    return lax.psum_scatter(
-        partial_out.astype(jnp.bfloat16), "col", scatter_dimension=0, tiled=True
-    )
+    return tail(cols, *projected, out_t, segment)
 
 
 def solution(mesh):

time: 303 us -> 283 us (0.934); the launches traced: 297 us -> 283 us
  Pallas kernels: 168 us -> 227 us
  waiting for transfers between devices: 45.2 us -> 0 us
  matrix products: 37.8 us -> 21.9 us
  between operations: 13.7 us -> 0.18 us
  local copies, waits for them, and re-layouts: 12.6 us -> 17.9 us
  other arithmetic: 19.9 us -> 15.6 us
    pallas_call x0 -> x1, Pallas kernels: none -> 59.6 us  [tail(): pl.pallas_call(functools.partial(tail_kernel, tuple(order)), out_shape=ja...]
    reduce_scatter x1 -> x0, waiting for transfers between devices: 45.2 us -> none  [on_device(): lax.psum_scatter(partial_out.astype(jnp.bfloat16), 'col', scatter_dimensi...]
    dot_general x33 -> x0, matrix products: 16.8 us -> none  [the longest x1 5.87 us: on_device(): lax.dot_general(attended, out_t, (((1,), (1,)), ((), ())), preferred_elem...]
    unnamed x21 -> x26, local copies, waits for them, and re-layouts: 7.56 us -> 11.9 us
    reduce_sum x16 -> x0, other arithmetic: 3.5 us -> none  [attend(): jnp.sum(exponent, axis=1, keepdims=True)]
  transfers between devices with their start and end apart: 1 -> 0, of which waited for: 1 -> 0; matrix products, arithmetic and copies ran while one was open for 0% -> 0% of each run, Pallas kernels for 0% -> 0%
where the time goes in v2:
time: 283 us
  Pallas kernels  227 us (80%)
  matrix products  21.9 us (8%)
  local copies, waits for them, and re-layouts  17.9 us (6%)
  other arithmetic  15.6 us (6%)
    pallas_call x1, Pallas kernels, move(): pl.pallas_call(functools.partial(move_kernel, row_n, col_n), out_shape=sh...  168 us
    pallas_call x1, Pallas kernels, tail(): pl.pallas_call(functools.partial(tail_kernel, tuple(order)), out_shape=ja...  59.6 us
    dot_general x3, matrix products, on_device(): jnp.dot(normed, parts[s], preferred_element_type=jnp.float32)  17.4 us
    unnamed x26, local copies, waits for them, and re-layouts  11.9 us
    convert_element_type x1, other arithmetic, on_device(): (floats * lax.rsqrt(mean_square + 1e-05) * norm_gain).astype(jnp.bfloat16)  10.3 us

profile of v2, /device:TPU:8, one launch (start us, length us, event | category | flops | bytes accessed | tf_op | source)
XLA Modules:
  0.0 282.8 jit_solution(14599176895459876211)
XLA Ops:
  0.0 0.0 copy-start
  0.0 1.9 copy.18
  1.9 1.4 copy.19
  3.3 1.8 copy.20
  5.1 0.0 copy-start.5
  5.1 1.3 copy.21
  6.4 1.8 copy.22
  8.3 1.3 copy.23
  9.6 0.0 copy-done.5
  9.6 0.1 convert_element_type.36
  9.7 0.8 copy.43
  10.5 167.6 %shard_map.91 = (bf16[1024,4096]{1,0:T(8,128)(2,1)}, bf16[32,128,512]{2,1,0:T(8,128)(2,1)}, bf16[32,128,512]{2,1,0:T(8,128)(2,1)}, bf16[32,128,512]{2,1,0:T(8,128)(2,1)}, bf16[32,64,512]{2,1,0:T(8,128)(2,1)}) custom-call(bf16[1024,512]{1,0:T(8,128)(2,1)} %x.1, bf16[8,128,512]{2,1,0:T(8,128)(2,1)} %bitcast.53, bf16[8,128,512]{2,1,0:T(8,128)(2,1)} %bitcast.54, ...), custom_call_target="tpu_custom_call" | custom-call | tf_op jit(solution)/shard_map/pallas_call | solution.py:477
  178.1 0.0 copy-start.7
  178.1 5.1 %fusion = f32[1024]{0:T(1024)S(1)} fusion(bf16[1024,4096]{1,0:T(8,128)(2,1)} %get-tuple-element.10), kind=kLoop, calls=%fused_computation.2 | loop fusion | flops 12581888 | bytes 8392704 | tf_op jit(solution)/shard_map/reduce_sum | solution.py:533
  183.2 0.0 copy-done.7
  183.2 10.3 %fusion.2 = bf16[1024,4096]{1,0:T(8,128)(2,1)} fusion(bf16[1024,4096]{1,0:T(8,128)(2,1)} %get-tuple-element.10, f32[4096]{0:T(1024)S(1)} %copy-done.7, f32[1024]{0:T(1024)S(1)} %add_rsqrt_fusion), kind=kLoop, calls=%fused_computation.4 | loop fusion | flops 16777216 | bytes 16797696 | tf_op jit(solution)/shard_map/convert_element_type | solution.py:534
  193.6 0.0 copy-start.4
  193.6 8.4 %fusion.12 = f32[1024,512]{1,0:T(8,128)S(1)} fusion(bf16[1024,4096]{1,0:T(8,128)(2,1)} %fusion.2, bf16[4096,512]{1,0:T(8,128)(2,1)} %bitcast.63), kind=kOutput, calls=%fused_computation.24 | convolution fusion | flops 4294967296 | bytes 14680064 | tf_op jit(solution)/shard_map/dot_general | solution.py:541
  202.0 0.0 copy-done
  202.0 0.0 copy-done.4
  202.1 0.0 copy-start.6
  202.1 2.3 convolution_convert_fusion
  204.4 0.0 copy-done.6
  204.4 0.0 copy-start.9
  204.4 0.1 fusion.9
  204.6 0.4 add_convert_fusion.values
  205.0 1.6 copy-done.9
  206.6 0.0 copy-start.8
  206.6 4.5 %fusion.11 = f32[1024,512]{1,0:T(8,128)S(1)} fusion(bf16[1024,4096]{1,0:T(8,128)(2,1)S(1)} %copy-done.4, bf16[4096,512]{1,0:T(8,128)(2,1)S(1)} %bitcast.62), kind=kOutput, calls=%fused_computation.23 | convolution fusion | flops 4294967296 | bytes 14680064 | tf_op jit(solution)/shard_map/dot_general | solution.py:541
  211.1 0.4 add_convert_fusion.1.keys
  211.5 0.0 copy-done.8
  211.5 0.0 copy-start.10
  211.5 4.5 %fusion.10 = f32[1024,512]{1,0:T(8,128)S(1)} fusion(bf16[1024,4096]{1,0:T(8,128)(2,1)S(1)} %copy-done.4, bf16[4096,512]{1,0:T(8,128)(2,1)S(1)} %bitcast.61), kind=kOutput, calls=%fused_computation.22 | convolution fusion | flops 4294967296 | bytes 14680064 | tf_op jit(solution)/shard_map/dot_general | solution.py:541
  216.0 1.4 add_convert_fusion.2.queries
  217.4 0.0 copy-done.10
  217.4 0.1 select_reduce_fusion
  217.5 0.1 convert_reduce_fusion
  217.6 1.0 copy.25.seg_col
  218.6 0.0 copy-start.1
  218.6 1.2 copy-done.1
  219.8 0.0 copy-start.2
  219.8 1.6 copy-done.2
  221.4 0.0 copy-start.3
  221.4 1.0 copy-done.3
  222.5 59.6 %shard_map.92 = bf16[128,2048]{1,0:T(8,128)(2,1)S(1)} custom-call(bf16[1024,512]{1,0:T(8,128)(2,1)S(1)} %copy-done.1, bf16[1024,512]{1,0:T(8,128)(2,1)S(1)} %add_convert_fusion.1.keys, bf16[1024,512]{1,0:T(8,128)(2,1)S(1)} %add_convert_fusion.values, bf16[2048,512]{1,0:T(8,128)(2,1)S(1)} %bitcast.47, s32[1024,1]{1,0:T(8,128)S(1)} %copy-done.3, ...), custom_call_target="tpu_custom_call" | custom-call | tf_op jit(solution)/shard_map/pallas_call | solution.py:220
  282.0 0.8 copy.45
  (1 shorter events, 0.0 us)
Async XLA Ops:
  0.0 202.0 %copy-start = (bf16[4096,128]{1,0:T(8,128)(2,1)S(1)}, bf16[4096,128]{1,0:T(8,128)(2,1)}, u32[]{:S(2)}) copy-start(bf16[4096,128]{1,0:T(8,128)(2,1)} %param.15) | copy-start | bytes 3145732
  5.1 4.5 %copy-start.5 = (f32[4096,64]{0,1:T(8,128)S(1)}, f32[4096,64]{0,1:T(8,128)}, u32[]{:S(2)}) copy-start(f32[4096,64]{0,1:T(8,128)} %param.14) | copy-start | bytes 3145732
  178.1 5.1 %copy-start.7 = (f32[4096]{0:T(1024)S(1)}, f32[4096]{0:T(1024)}, u32[]{:S(2)}) copy-start(f32[4096]{0:T(1024)} %param.10) | copy-start | bytes 49156
  193.6 8.5 %copy-start.4 = (bf16[1024,4096]{1,0:T(8,128)(2,1)S(1)}, bf16[1024,4096]{1,0:T(8,128)(2,1)}, u32[]{:S(2)}) copy-start(bf16[1024,4096]{1,0:T(8,128)(2,1)} %fusion.2) | copy-start | bytes 25165828
  202.1 2.3 copy-start.6
  204.4 2.2 copy-start.9
  206.6 4.9 %copy-start.8 = (bf16[32,128,512]{2,1,0:T(8,128)(2,1)S(1)}, bf16[32,128,512]{2,1,0:T(8,128)(2,1)}, u32[]{:S(2)}) copy-start(bf16[32,128,512]{2,1,0:T(8,128)(2,1)} %get-tuple-element.11) | copy-start | bytes 12582916
  211.5 5.9 %copy-start.10 = (s32[1,7]{1,0:T(1,128)S(1)}, s32[1,7]{1,0:T(1,128)}, u32[]{:S(2)}) copy-start(s32[1,7]{1,0:T(1,128)} %param.17) | copy-start | bytes 88
  218.6 1.2 copy-start.1
  219.8 1.6 copy-start.2
  221.4 1.0 copy-start.3
